TPU v7x, 512 devices: a whole 4x8x8 slice. The times are simulated.
512 devices in a mesh: area: 128 (over z, y, core), nrn: 4 (over x).
Axes of the slice: x: 4, y: 8, z: 8, core: 2. Of those that a mesh axis runs over, the one named last changes fastest.
Arguments:
- history: float32 [4, 65536, 128], P(None, ('area', 'nrn')), may hold values from -1 to 1
- drive: float32 [65536, 128], P(('area', 'nrn')), may hold values from -6 to 6
- leak: float32 [65536], P(('area', 'nrn')), may hold values from 0.1 to 0.9
- w_local: float32 [65536, 512], P(('area', 'nrn')), may hold values from -0.25 to 0.25
- w_long: float32 [65536, 4, 1152], P(('area', 'nrn')), may hold values from -0.1875 to 0.1875
- sender_rows: int32 [512, 128, 9], P(('area', 'nrn')), may hold values from 0 to 127
- delays: int32 [128, 128], P('area'), may hold values from 1 to 4
- area_sizes: int32 [128], P('area'), may hold values from 256 to 512, as said below
Outputs:
- rates: float32 [65536, 128], P(('area', 'nrn'))
Inputs may be any that keep to these rules, and one draw needn't show every extreme that they name: `area_sizes`: every area has at least half of its 512 slots live; some area has all of them live, some exactly half. `sender_rows`: indices may repeat.
All inputs are finite; a program needn't handle non-finite values.
Results may differ from a plain program's by a relative error of at most 0.0018.
Values may be sent and summed in bfloat16 or wider, within the bound.
A program may use at most 64 MiB of HBM per device.

v0:
```python
import jax
import jax.numpy as jnp
from jax import lax
from jax.sharding import PartitionSpec as P

STEPS = 6


def cut_along(x, dim, peers):
    lengths = x.shape
    pieces = x.reshape(*lengths[:dim], peers, lengths[dim] // peers, *lengths[dim + 1 :])
    return jnp.moveaxis(pieces, dim, 0)


def sum_at_owner(x, axis, dim):
    peers = lax.axis_size(axis)
    pieces = lax.all_to_all(cut_along(x, dim, peers), axis, 0, 0, tiled=True)
    return jnp.sum(pieces, axis=0)


def unround(values):
    return lax.optimization_barrier(values).astype(jnp.float32)


def local(history, drive, leak, w_local, w_long, sender_rows, delays, area_sizes):
    history_depth, block_rows, stimuli = history.shape
    nrn_count = lax.axis_size("nrn")
    area_count = sender_rows.shape[1]
    proj_count = sender_rows.shape[2]
    offsets = lax.axis_index("nrn") * block_rows + jnp.arange(block_rows, dtype=jnp.int32)
    active = (offsets < area_sizes[0]).astype(jnp.float32)[:, None]
    states = history * active[None]
    picked = ((delays[0] - 1)[:, None] * block_rows + sender_rows[0]).reshape(-1)
    grouped = lax.all_to_all(w_long, "nrn", split_axis=1, concat_axis=0, tiled=True).reshape(
        nrn_count * block_rows, -1
    )
    for iteration in range(STEPS):
        flat_states = states.reshape(history_depth * block_rows, stimuli)
        outgoing = flat_states[picked].astype(jnp.bfloat16).reshape(area_count, proj_count, stimuli)
        incoming = lax.all_to_all(outgoing, "area", split_axis=0, concat_axis=0, tiled=True)
        current = states[0].astype(jnp.bfloat16)
        local_all = lax.all_gather(current, "nrn", axis=0, tiled=True)
        sources = unround(incoming).reshape(-1, stimuli)
        long_term = sum_at_owner(
            jnp.dot(
                grouped,
                sources,
                precision=lax.Precision.HIGHEST,
                preferred_element_type=jnp.float32,
            ),
            "nrn",
            0,
        )
        inputs = (
            long_term
            + jnp.dot(
                w_local,
                unround(local_all),
                precision=lax.Precision.HIGHEST,
                preferred_element_type=jnp.float32,
            )
            + drive
        )
        updated = active * (states[0] + leak[:, None] * (jnp.tanh(inputs) - states[0]))
        states = jnp.concatenate([updated[None], states[:-1]], axis=0)
    return states[0]


def solution(mesh):
    placed = (
        P(None, ("area", "nrn"), None),
        P(("area", "nrn"), None),
        P(("area", "nrn")),
        P(("area", "nrn"), None),
        P(("area", "nrn"), None, None),
        P(("area", "nrn"), None, None),
        P("area", None),
        P("area"),
    )
    return jax.shard_map(
        local, mesh=mesh, in_specs=placed, out_specs=P(("area", "nrn"), None), check_vma=False
    )
```

profile of v0, /device:TPU:8, one launch (start us, length us, event | category | flops | bytes accessed | tf_op | source)
XLA Modules:
  0.0 353.5 jit_solution(10322337798542457753)
XLA Ops:
  1.7 0.8 copy.13
  2.7 1.0 broadcast_multiply_fusion
  3.8 2.5 gather_fusion
  6.3 0.9 convert_element_type.85
  7.2 17.4 %all-to-all-start = ((bf16[128,9,128]{2,1,0:T(8,128)(2,1)}), bf16[128,9,128]{2,1,0:T(8,128)(2,1)S(1)}, u32[]{:S(2)}, u32[]{:S(2)}) async-start(bf16[128,9,128]{2,1,0:T(8,128)(2,1)} %convert_element_type.85), calls=%async_computation | async-start | bytes 1048576 | tf_op jit(solution)/shard_map/all_to_all | solution.py:40
  24.6 1.6 copy.14
  26.2 18.6 %all-to-all-done = bf16[128,9,128]{2,1,0:T(8,128)(2,1)S(1)} async-done(((bf16[128,9,128]{2,1,0:T(8,128)(2,1)}), bf16[128,9,128]{2,1,0:T(8,128)(2,1)S(1)}, u32[]{:S(2)}, u32[]{:S(2)}) %all-to-all-start) | async-done | bytes 294944 | tf_op jit(solution)/shard_map/all_to_all | solution.py:40
  44.8 4.3 %all-to-all-start.1 = ((f32[128,4,1152]{2,0,1:T(8,128)}), f32[128,4,1152]{2,0,1:T(8,128)S(1)}, u32[]{:S(2)}, u32[]{:S(2)}) async-start(f32[128,4,1152]{2,0,1:T(8,128)} %copy.14), calls=%async_computation.1 | async-start | bytes 4718592 | tf_op jit(solution)/shard_map/all_to_all | solution.py:34
  49.7 0.9 reshape.130
  50.6 27.7 %all-to-all-done.1 = f32[128,4,1152]{2,0,1:T(8,128)S(1)} async-done(((f32[128,4,1152]{2,0,1:T(8,128)}), f32[128,4,1152]{2,0,1:T(8,128)S(1)}, u32[]{:S(2)}, u32[]{:S(2)}) %all-to-all-start.1) | async-done | bytes 2359328 | tf_op jit(solution)/shard_map/all_to_all | solution.py:34
  78.3 2.4 convolution_bitcast_fusion.5
  81.5 3.4 all-to-all-start.2
  84.9 13.0 %all_gather.18 = bf16[512,128]{1,0:T(8,128)(2,1)S(1)} all-gather(bf16[128,128]{1,0:T(8,128)(2,1)S(1)} %fusion.46), channel_id=1, replica_groups=mesh['area'=128,'nrn'=4] {'nrn'}, dimensions={0}, use_global_device_ids=true | all-gather | bytes 163840 | tf_op jit(solution)/shard_map/all_gather | solution.py:42
  99.0 2.9 gather_fusion.1
  102.0 27.2 %all_to_all.75 = bf16[128,9,128]{2,1,0:T(8,128)(2,1)} all-to-all(bf16[128,9,128]{2,1,0:T(8,128)(2,1)S(1)} %convert_element_type.88), channel_id=1, replica_groups=mesh['area'=128,'nrn'=4] {'area'}, dimensions={0} | all-to-all | bytes 589824 | tf_op jit(solution)/shard_map/all_to_all | solution.py:40
  129.2 1.2 reshape.134
  130.4 1.5 convolution_bitcast_fusion.4
  132.6 3.4 all-to-all-start.4
  136.0 13.8 %all_gather.19 = bf16[512,128]{1,0:T(8,128)(2,1)S(1)} all-gather(bf16[128,128]{1,0:T(8,128)(2,1)S(1)} %get-tuple-element.5), channel_id=1, replica_groups=mesh['area'=128,'nrn'=4] {'nrn'}, dimensions={0}, use_global_device_ids=true | all-gather | bytes 163840 | tf_op jit(solution)/shard_map/all_gather | solution.py:42
  150.9 2.9 gather_fusion.2
  154.0 25.9 %all_to_all.76 = bf16[128,9,128]{2,1,0:T(8,128)(2,1)} all-to-all(bf16[128,9,128]{2,1,0:T(8,128)(2,1)S(1)} %convert_element_type.91), channel_id=1, replica_groups=mesh['area'=128,'nrn'=4] {'area'}, dimensions={0} | all-to-all | bytes 589824 | tf_op jit(solution)/shard_map/all_to_all | solution.py:40
  179.9 1.2 reshape.137
  181.1 1.5 convolution_bitcast_fusion.3
  182.6 0.7 copy.56
  183.3 3.4 all-to-all-start.6
  186.7 13.8 %all_gather.20 = bf16[512,128]{1,0:T(8,128)(2,1)S(1)} all-gather(bf16[128,128]{1,0:T(8,128)(2,1)S(1)} %get-tuple-element.7), channel_id=1, replica_groups=mesh['area'=128,'nrn'=4] {'nrn'}, dimensions={0}, use_global_device_ids=true | all-gather | bytes 163840 | tf_op jit(solution)/shard_map/all_gather | solution.py:42
  201.6 2.9 gather_fusion.3
  204.6 25.9 %all_to_all.77 = bf16[128,9,128]{2,1,0:T(8,128)(2,1)} all-to-all(bf16[128,9,128]{2,1,0:T(8,128)(2,1)S(1)} %convert_element_type.94), channel_id=1, replica_groups=mesh['area'=128,'nrn'=4] {'area'}, dimensions={0} | all-to-all | bytes 589824 | tf_op jit(solution)/shard_map/all_to_all | solution.py:40
  230.6 1.2 reshape.140
  231.8 1.5 convolution_bitcast_fusion.2
  233.3 0.7 copy.55
  234.0 3.4 all-to-all-start.8
  237.4 13.8 %all_gather.21 = bf16[512,128]{1,0:T(8,128)(2,1)S(1)} all-gather(bf16[128,128]{1,0:T(8,128)(2,1)S(1)} %get-tuple-element.9), channel_id=1, replica_groups=mesh['area'=128,'nrn'=4] {'nrn'}, dimensions={0}, use_global_device_ids=true | all-gather | bytes 163840 | tf_op jit(solution)/shard_map/all_gather | solution.py:42
  252.3 2.9 gather_fusion.4
  255.3 25.9 %all_to_all.78 = bf16[128,9,128]{2,1,0:T(8,128)(2,1)} all-to-all(bf16[128,9,128]{2,1,0:T(8,128)(2,1)S(1)} %convert_element_type.97), channel_id=1, replica_groups=mesh['area'=128,'nrn'=4] {'area'}, dimensions={0} | all-to-all | bytes 589824 | tf_op jit(solution)/shard_map/all_to_all | solution.py:40
  281.3 1.2 reshape.143
  282.5 1.5 convolution_bitcast_fusion.1
  283.9 0.7 copy.54
  284.7 3.4 all-to-all-start.10
  288.1 13.7 %all_gather.22 = bf16[512,128]{1,0:T(8,128)(2,1)S(1)} all-gather(bf16[128,128]{1,0:T(8,128)(2,1)S(1)} %get-tuple-element.11), channel_id=1, replica_groups=mesh['area'=128,'nrn'=4] {'nrn'}, dimensions={0}, use_global_device_ids=true | all-gather | bytes 163840 | tf_op jit(solution)/shard_map/all_gather | solution.py:42
  302.9 2.9 gather_fusion.5
  305.9 25.9 %all_to_all.79 = bf16[128,9,128]{2,1,0:T(8,128)(2,1)} all-to-all(bf16[128,9,128]{2,1,0:T(8,128)(2,1)S(1)} %convert_element_type.100), channel_id=1, replica_groups=mesh['area'=128,'nrn'=4] {'area'}, dimensions={0} | all-to-all | bytes 589824 | tf_op jit(solution)/shard_map/all_to_all | solution.py:40
  331.8 1.2 reshape.146
  333.0 1.5 convolution_bitcast_fusion
  334.5 0.7 copy.53
  335.2 3.4 all-to-all-start.12
  338.6 13.8 %all_gather.23 = bf16[512,128]{1,0:T(8,128)(2,1)S(1)} all-gather(bf16[128,128]{1,0:T(8,128)(2,1)S(1)} %get-tuple-element.13), channel_id=1, replica_groups=mesh['area'=128,'nrn'=4] {'nrn'}, dimensions={0}, use_global_device_ids=true | all-gather | bytes 163840 | tf_op jit(solution)/shard_map/all_gather | solution.py:42
  352.6 0.9 fusion.41
  (92 shorter events, 9.1 us)
Async XLA Ops:
  0.0 98.0 %copy-start = (f32[128,512]{1,0:T(8,128)S(1)}, f32[128,512]{1,0:T(8,128)}, u32[]{:S(2)}) copy-start(f32[128,512]{1,0:T(8,128)} %param.11) | copy-start | bytes 786436
  3.8 20.8 %copy-start.1 = (f32[128,4,1152]{2,1,0:T(4,128)S(1)}, f32[128,4,1152]{2,1,0:T(4,128)}, u32[]{:S(2)}) copy-start(f32[128,4,1152]{2,1,0:T(4,128)} %param.12) | copy-start | bytes 7077892
  7.2 37.6 %all-to-all-start = ((bf16[128,9,128]{2,1,0:T(8,128)(2,1)}), bf16[128,9,128]{2,1,0:T(8,128)(2,1)S(1)}, u32[]{:S(2)}, u32[]{:S(2)}) async-start(bf16[128,9,128]{2,1,0:T(8,128)(2,1)} %convert_element_type.85), calls=%async_computation | async-start | bytes 1048576 | tf_op jit(solution)/shard_map/all_to_all | solution.py:40
  44.8 33.5 %all-to-all-start.1 = ((f32[128,4,1152]{2,0,1:T(8,128)}), f32[128,4,1152]{2,0,1:T(8,128)S(1)}, u32[]{:S(2)}, u32[]{:S(2)}) async-start(f32[128,4,1152]{2,0,1:T(8,128)} %copy.14), calls=%async_computation.1 | async-start | bytes 4718592 | tf_op jit(solution)/shard_map/all_to_all | solution.py:34
  50.6 47.4 %copy-start.2 = (f32[128,128]{1,0:T(8,128)S(1)}, f32[128,128]{1,0:T(8,128)}, u32[]{:S(2)}) copy-start(f32[128,128]{1,0:T(8,128)} %param.9) | copy-start | bytes 196612
  50.6 47.4 %copy-start.21 = (f32[128]{0:T(128)S(1)}, f32[128]{0:T(128)}, u32[]{:S(2)}) copy-start(f32[128]{0:T(128)} %param.10) | copy-start | bytes 1540
  78.3 20.0 %copy-start.11 = (bf16[3,128,128]{2,1,0:T(8,128)(2,1)S(1)}, bf16[3,128,128]{2,1,0:T(8,128)(2,1)}, u32[]{:S(2)}) copy-start(bf16[3,128,128]{2,1,0:T(8,128)(2,1)} %slice.39) | copy-start | bytes 294916
  81.5 16.4 %all-to-all-start.2 = ((f32[4,128,128]{1,2,0:T(8,128)}), f32[4,128,128]{1,2,0:T(8,128)S(1)}, u32[]{:S(2)}, u32[]{:S(2)}) async-start(f32[4,128,128]{1,2,0:T(8,128)} %bitcast.180), calls=%async_computation.2 | async-start | bytes 524288 | tf_op jit(solution)/shard_map/all_to_all | solution.py:17
  98.3 0.6 copy-start.3
  129.2 20.6 %copy-start.4 = (f32[128,128]{1,0:T(8,128)S(1)}, f32[128,128]{1,0:T(8,128)}, u32[]{:S(2)}) copy-start(f32[128,128]{1,0:T(8,128)} %copy-done.3) | copy-start | bytes 196612
  129.2 20.6 %copy-start.12 = (bf16[3,128,128]{2,1,0:T(8,128)(2,1)S(1)}, bf16[3,128,128]{2,1,0:T(8,128)(2,1)}, u32[]{:S(2)}) copy-start(bf16[3,128,128]{2,1,0:T(8,128)(2,1)} %slice.39) | copy-start | bytes 294916
  132.6 17.3 %all-to-all-start.4 = ((f32[4,128,128]{1,2,0:T(8,128)}), f32[4,128,128]{1,2,0:T(8,128)S(1)}, u32[]{:S(2)}, u32[]{:S(2)}) async-start(f32[4,128,128]{1,2,0:T(8,128)} %bitcast.179), calls=%async_computation.4 | async-start | bytes 524288 | tf_op jit(solution)/shard_map/all_to_all | solution.py:17
  149.8 0.6 copy-start.13
  150.3 0.6 copy-start.5
  179.9 20.6 %copy-start.6 = (f32[128,128]{1,0:T(8,128)S(1)}, f32[128,128]{1,0:T(8,128)}, u32[]{:S(2)}) copy-start(f32[128,128]{1,0:T(8,128)} %copy-done.5) | copy-start | bytes 196612
  179.9 20.6 %copy-start.14 = (bf16[3,128,128]{2,1,0:T(8,128)(2,1)S(1)}, bf16[3,128,128]{2,1,0:T(8,128)(2,1)}, u32[]{:S(2)}) copy-start(bf16[3,128,128]{2,1,0:T(8,128)(2,1)} %copy-done.13) | copy-start | bytes 294916
  183.3 17.2 %all-to-all-start.6 = ((f32[4,128,128]{1,2,0:T(8,128)}), f32[4,128,128]{1,2,0:T(8,128)S(1)}, u32[]{:S(2)}, u32[]{:S(2)}) async-start(f32[4,128,128]{1,2,0:T(8,128)} %bitcast.178), calls=%async_computation.6 | async-start | bytes 524288 | tf_op jit(solution)/shard_map/all_to_all | solution.py:17
  200.5 0.6 copy-start.15
  200.9 0.6 copy-start.7
  230.6 20.6 %copy-start.8 = (f32[128,128]{1,0:T(8,128)S(1)}, f32[128,128]{1,0:T(8,128)}, u32[]{:S(2)}) copy-start(f32[128,128]{1,0:T(8,128)} %copy-done.7) | copy-start | bytes 196612
  230.6 20.6 %copy-start.16 = (bf16[3,128,128]{2,1,0:T(8,128)(2,1)S(1)}, bf16[3,128,128]{2,1,0:T(8,128)(2,1)}, u32[]{:S(2)}) copy-start(bf16[3,128,128]{2,1,0:T(8,128)(2,1)} %copy-done.15) | copy-start | bytes 294916
  234.0 17.2 %all-to-all-start.8 = ((f32[4,128,128]{1,2,0:T(8,128)}), f32[4,128,128]{1,2,0:T(8,128)S(1)}, u32[]{:S(2)}, u32[]{:S(2)}) async-start(f32[4,128,128]{1,2,0:T(8,128)} %bitcast.177), calls=%async_computation.8 | async-start | bytes 524288 | tf_op jit(solution)/shard_map/all_to_all | solution.py:17
  251.2 0.6 copy-start.17
  251.6 0.6 copy-start.9
  281.3 20.5 %copy-start.10 = (f32[128,128]{1,0:T(8,128)S(1)}, f32[128,128]{1,0:T(8,128)}, u32[]{:S(2)}) copy-start(f32[128,128]{1,0:T(8,128)} %copy-done.9) | copy-start | bytes 196612
  281.3 20.5 %copy-start.18 = (bf16[3,128,128]{2,1,0:T(8,128)(2,1)S(1)}, bf16[3,128,128]{2,1,0:T(8,128)(2,1)}, u32[]{:S(2)}) copy-start(bf16[3,128,128]{2,1,0:T(8,128)(2,1)} %copy-done.17) | copy-start | bytes 294916
  284.7 17.2 %all-to-all-start.10 = ((f32[4,128,128]{1,2,0:T(8,128)}), f32[4,128,128]{1,2,0:T(8,128)S(1)}, u32[]{:S(2)}, u32[]{:S(2)}) async-start(f32[4,128,128]{1,2,0:T(8,128)} %bitcast.176), calls=%async_computation.10 | async-start | bytes 524288 | tf_op jit(solution)/shard_map/all_to_all | solution.py:17
  302.2 0.6 copy-start.19
  333.0 19.5 %copy-start.20 = (f32[128,128]{1,0:T(8,128)S(1)}, f32[128,128]{1,0:T(8,128)}, u32[]{:S(2)}) copy-start(f32[128,128]{1,0:T(8,128)} %copy-done.19) | copy-start | bytes 196612
  335.2 17.2 %all-to-all-start.12 = ((f32[4,128,128]{1,2,0:T(8,128)}), f32[4,128,128]{1,2,0:T(8,128)S(1)}, u32[]{:S(2)}, u32[]{:S(2)}) async-start(f32[4,128,128]{1,2,0:T(8,128)} %bitcast.175), calls=%async_computation.12 | async-start | bytes 524288 | tf_op jit(solution)/shard_map/all_to_all | solution.py:17
where the time goes:
time: 355 us; the launch traced here: 353 us
  blocking collectives  213 us (60%)
  waiting for transfers between devices  46.3 us (13%)
  starting transfers between devices  42.1 us (12%)
  local copies, waits for them, and re-layouts  37 us (10%)
  matrix products  12 us (3%)
    all_to_all x5, blocking collectives, local(): lax.all_to_all(outgoing, 'area', split_axis=0, concat_axis=0, tiled=True)  131 us
    all_gather x6, blocking collectives, local(): local_all = lax.all_gather(current, 'nrn', axis=0, tiled=True)  81.9 us
    all_to_all x1, waiting for transfers between devices, local(): lax.all_to_all(w_long, 'nrn', split_axis=1, concat_axis=0, tiled=True)  27.7 us
    all_to_all x6, starting transfers between devices, sum_at_owner(): pieces = lax.all_to_all(cut_along(x, dim, peers), axis, 0, 0, tiled=True)  20.4 us
    all_to_all x1, waiting for transfers between devices, local(): lax.all_to_all(outgoing, 'area', split_axis=0, concat_axis=0, tiled=True)  18.6 us
    all_to_all x1, starting transfers between devices, local(): lax.all_to_all(outgoing, 'area', split_axis=0, concat_axis=0, tiled=True)  17.4 us
    gather x6, local copies, waits for them, and re-layouts, local(): flat_states[picked].astype(jnp.bfloat16)  17.1 us
    dot_general x6, matrix products, local(): jnp.dot(grouped, sources, precision=lax.Precision.HIGHEST, preferred_elem...  9.74 us
  transfers between devices with their start and end apart: 8, of which 2 were waited for; matrix products, arithmetic and copies ran while one was open for 1% of the time, Pallas kernels for 0%

commit v1 on v0

--- a/solution.py
+++ b/solution.py
@@ -4,6 +4,12 @@
 from jax.sharding import PartitionSpec as P
 
 STEPS = 6
+
+
+def joined_along(parts, dim):
+    parts = jnp.moveaxis(parts, 0, dim)
+    lengths = parts.shape
+    return parts.reshape(*lengths[:dim], lengths[dim] * lengths[dim + 1], *lengths[dim + 2 :])
 
 
 def cut_along(x, dim, peers):
@@ -39,7 +45,19 @@
         outgoing = flat_states[picked].astype(jnp.bfloat16).reshape(area_count, proj_count, stimuli)
         incoming = lax.all_to_all(outgoing, "area", split_axis=0, concat_axis=0, tiled=True)
         current = states[0].astype(jnp.bfloat16)
-        local_all = lax.all_gather(current, "nrn", axis=0, tiled=True)
+        peers_2 = lax.axis_size("nrn")
+        pairs = [(i, (i + 1) % peers_2) for i in range(peers_2)]
+        back = [(b, a) for a, b in pairs]
+        lower, upper = ([], [])
+        for turn in range(peers_2 - 1):
+            if turn % 2 == 0:
+                lower.append(lax.ppermute(lower[-1] if lower else current, "nrn", pairs))
+            else:
+                upper.append(lax.ppermute(upper[-1] if upper else current, "nrn", back))
+        blocks = jnp.stack([*lower[::-1], current, *upper])
+        shift = lax.axis_index("nrn") - len(lower)
+        blocks = blocks[(jnp.arange(peers_2) - shift) % peers_2]
+        local_all = joined_along(blocks, 0)
         sources = unround(incoming).reshape(-1, stimuli)
         long_term = sum_at_owner(
             jnp.dot(

time: 355 us -> 330 us (0.930)
  the two profiles are of different devices: /device:TPU:8 before, /device:TPU:1 now
where the time goes in v1:
time: 330 us; the launch traced here: 328 us
  starting transfers between devices  122 us (37%)
  waiting for transfers between devices  118 us (36%)
  local copies, waits for them, and re-layouts  39.9 us (12%)
  blocking collectives  26.3 us (8%)
  matrix products  12.9 us (4%)
  other arithmetic  6.66 us (2%)
    all_to_all x5, waiting for transfers between devices, local(): lax.all_to_all(outgoing, 'area', split_axis=0, concat_axis=0, tiled=True)  67.7 us
    all_to_all x5, starting transfers between devices, local(): lax.all_to_all(outgoing, 'area', split_axis=0, concat_axis=0, tiled=True)  43.9 us
    ppermute x12, starting transfers between devices, local(): lower.append(lax.ppermute(lower[-1] if lower else current, 'nrn', pairs))  28 us
    all_to_all x1, blocking collectives, local(): lax.all_to_all(outgoing, 'area', split_axis=0, concat_axis=0, tiled=True)  26.3 us
    all_to_all x6, waiting for transfers between devices, sum_at_owner(): pieces = lax.all_to_all(cut_along(x, dim, peers), axis, 0, 0, tiled=True)  25.6 us
    ppermute x6, starting transfers between devices, local(): upper.append(lax.ppermute(upper[-1] if upper else current, 'nrn', back))  25 us
    ppermute x12, waiting for transfers between devices, local(): lower.append(lax.ppermute(lower[-1] if lower else current, 'nrn', pairs))  24.9 us
    all_to_all x6, starting transfers between devices, sum_at_owner(): pieces = lax.all_to_all(cut_along(x, dim, peers), axis, 0, 0, tiled=True)  21 us
  transfers between devices with their start and end apart: 30, of which 13 were waited for; matrix products, arithmetic and copies ran while one was open for 7% of the time, Pallas kernels for 0%

profile of v1, /device:TPU:1, one launch (start us, length us, event | category | flops | bytes accessed | tf_op | source)
XLA Modules:
  0.0 327.6 jit_solution(13052577272770913790)
XLA Ops:
  3.8 2.5 gather_fusion
  7.2 18.4 %all-to-all-start = ((bf16[128,9,128]{2,1,0:T(8,128)(2,1)}), bf16[128,9,128]{2,1,0:T(8,128)(2,1)S(1)}, u32[]{:S(2)}, u32[]{:S(2)}) async-start(bf16[128,9,128]{2,1,0:T(8,128)(2,1)} %convert_element_type.88), calls=%async_computation | async-start | bytes 1048576 | tf_op jit(solution)/shard_map/all_to_all | solution.py:46
  27.2 19.0 %all-to-all-done = bf16[128,9,128]{2,1,0:T(8,128)(2,1)S(1)} async-done(((bf16[128,9,128]{2,1,0:T(8,128)(2,1)}), bf16[128,9,128]{2,1,0:T(8,128)(2,1)S(1)}, u32[]{:S(2)}, u32[]{:S(2)}) %all-to-all-start) | async-done | bytes 294944 | tf_op jit(solution)/shard_map/all_to_all | solution.py:46
  46.2 4.0 %all-to-all-start.1 = ((f32[128,4,1152]{2,0,1:T(8,128)}), f32[128,4,1152]{2,0,1:T(8,128)S(1)}, u32[]{:S(2)}, u32[]{:S(2)}) async-start(f32[128,4,1152]{2,0,1:T(8,128)} %copy.14), calls=%async_computation.1 | async-start | bytes 4718592 | tf_op jit(solution)/shard_map/all_to_all | solution.py:40
  50.2 4.6 %collective-permute-start.2 = (bf16[128,128]{1,0:T(8,128)(2,1)S(1)}, bf16[128,128]{1,0:T(8,128)(2,1)}, u32[]{:S(2)}, u32[]{:S(2)}) collective-permute-start(bf16[128,128]{1,0:T(8,128)(2,1)S(1)} %get-tuple-element.6), channel_id=1, source_target_pairs={{1,0},{2,1},{3,2},{0,3},{5,4},{6,5},{7,6},{4,7},{9,8},{10,9},{11,1... | collective-permute-start | bytes 98312 | tf_op jit(solution)/shard_map/ppermute | solution.py:56
  54.8 1.9 collective-permute-start
  57.3 19.6 %collective-permute-done = bf16[128,128]{1,0:T(8,128)(2,1)} collective-permute-done((bf16[128,128]{1,0:T(8,128)(2,1)S(1)}, bf16[128,128]{1,0:T(8,128)(2,1)}, u32[]{:S(2)}, u32[]{:S(2)}) %collective-permute-start) | collective-permute-done | bytes 32800 | tf_op jit(solution)/shard_map/ppermute | solution.py:54
  76.9 4.2 %collective-permute-start.1 = (bf16[128,128]{1,0:T(8,128)(2,1)}, bf16[128,128]{1,0:T(8,128)(2,1)}, u32[]{:S(2)}, u32[]{:S(2)}) collective-permute-start(bf16[128,128]{1,0:T(8,128)(2,1)} %collective-permute-done), channel_id=1, source_target_pairs={{0,1},{1,2},{2,3},{3,0},{4,5},{5,6},{6,7},{7,4},{8,9},{9,10},{10,1... | collective-permute-start | bytes 98312 | tf_op jit(solution)/shard_map/ppermute | solution.py:54
  82.0 2.4 convolution_bitcast_fusion.5
  85.2 4.0 %all-to-all-start.2 = ((f32[4,128,128]{1,2,0:T(8,128)}), f32[4,128,128]{1,2,0:T(8,128)S(1)}, u32[]{:S(2)}, u32[]{:S(2)}) async-start(f32[4,128,128]{1,2,0:T(8,128)} %bitcast.208), calls=%async_computation.2 | async-start | bytes 524288 | tf_op jit(solution)/shard_map/all_to_all | solution.py:23
  91.2 3.4 %all-to-all-done.2 = f32[4,128,128]{1,2,0:T(8,128)S(1)} async-done(((f32[4,128,128]{1,2,0:T(8,128)}), f32[4,128,128]{1,2,0:T(8,128)S(1)}, u32[]{:S(2)}, u32[]{:S(2)}) %all-to-all-start.2) | async-done | bytes 262176 | tf_op jit(solution)/shard_map/all_to_all | solution.py:23
  96.6 2.9 gather_fusion.2
  100.5 8.5 %all-to-all-start.3 = ((bf16[128,9,128]{2,1,0:T(8,128)(2,1)}), bf16[128,9,128]{2,1,0:T(8,128)(2,1)S(1)}, u32[]{:S(2)}, u32[]{:S(2)}) async-start(bf16[128,9,128]{2,1,0:T(8,128)(2,1)} %convert_element_type.92), calls=%async_computation.3 | async-start | bytes 1048576 | tf_op jit(solution)/shard_map/all_to_all | solution.py:46
  108.9 2.2 collective-permute-start.3
  111.2 4.3 %collective-permute-start.5 = (bf16[128,128]{1,0:T(8,128)(2,1)S(1)}, bf16[128,128]{1,0:T(8,128)(2,1)}, u32[]{:S(2)}, u32[]{:S(2)}) collective-permute-start(bf16[128,128]{1,0:T(8,128)(2,1)S(1)} %get-tuple-element.7), channel_id=1, source_target_pairs={{1,0},{2,1},{3,2},{0,3},{5,4},{6,5},{7,6},{4,7},{9,8},{10,9},{11,1... | collective-permute-start | bytes 98312 | tf_op jit(solution)/shard_map/ppermute | solution.py:56
  115.5 1.9 collective-permute-start.4
  117.4 12.2 %all-to-all-done.3 = bf16[128,9,128]{2,1,0:T(8,128)(2,1)S(1)} async-done(((bf16[128,9,128]{2,1,0:T(8,128)(2,1)}), bf16[128,9,128]{2,1,0:T(8,128)(2,1)S(1)}, u32[]{:S(2)}, u32[]{:S(2)}) %all-to-all-start.3) | async-done | bytes 294944 | tf_op jit(solution)/shard_map/all_to_all | solution.py:46
  132.0 3.4 %all-to-all-start.4 = ((f32[4,128,128]{1,2,0:T(8,128)}), f32[4,128,128]{1,2,0:T(8,128)S(1)}, u32[]{:S(2)}, u32[]{:S(2)}) async-start(f32[4,128,128]{1,2,0:T(8,128)} %bitcast.207), calls=%async_computation.4 | async-start | bytes 524288 | tf_op jit(solution)/shard_map/all_to_all | solution.py:23
  137.0 5.5 %all-to-all-done.4 = f32[4,128,128]{1,2,0:T(8,128)S(1)} async-done(((f32[4,128,128]{1,2,0:T(8,128)}), f32[4,128,128]{1,2,0:T(8,128)S(1)}, u32[]{:S(2)}, u32[]{:S(2)}) %all-to-all-start.4) | async-done | bytes 262176 | tf_op jit(solution)/shard_map/all_to_all | solution.py:23
  143.6 2.9 gather_fusion.4
  147.4 5.8 %all-to-all-start.5 = ((bf16[128,9,128]{2,1,0:T(8,128)(2,1)}), bf16[128,9,128]{2,1,0:T(8,128)(2,1)S(1)}, u32[]{:S(2)}, u32[]{:S(2)}) async-start(bf16[128,9,128]{2,1,0:T(8,128)(2,1)} %convert_element_type.95), calls=%async_computation.5 | async-start | bytes 1048576 | tf_op jit(solution)/shard_map/all_to_all | solution.py:46
  153.2 2.2 collective-permute-start.6
  155.4 4.3 %collective-permute-start.8 = (bf16[128,128]{1,0:T(8,128)(2,1)S(1)}, bf16[128,128]{1,0:T(8,128)(2,1)}, u32[]{:S(2)}, u32[]{:S(2)}) collective-permute-start(bf16[128,128]{1,0:T(8,128)(2,1)S(1)} %get-tuple-element.9), channel_id=1, source_target_pairs={{1,0},{2,1},{3,2},{0,3},{5,4},{6,5},{7,6},{4,7},{9,8},{10,9},{11,1... | collective-permute-start | bytes 98312 | tf_op jit(solution)/shard_map/ppermute | solution.py:56
  159.7 1.9 collective-permute-start.7
  161.7 12.2 %all-to-all-done.5 = bf16[128,9,128]{2,1,0:T(8,128)(2,1)S(1)} async-done(((bf16[128,9,128]{2,1,0:T(8,128)(2,1)}), bf16[128,9,128]{2,1,0:T(8,128)(2,1)S(1)}, u32[]{:S(2)}, u32[]{:S(2)}) %all-to-all-start.5) | async-done | bytes 294944 | tf_op jit(solution)/shard_map/all_to_all | solution.py:46
  176.2 3.4 %all-to-all-start.6 = ((f32[4,128,128]{1,2,0:T(8,128)}), f32[4,128,128]{1,2,0:T(8,128)S(1)}, u32[]{:S(2)}, u32[]{:S(2)}) async-start(f32[4,128,128]{1,2,0:T(8,128)} %bitcast.206), calls=%async_computation.6 | async-start | bytes 524288 | tf_op jit(solution)/shard_map/all_to_all | solution.py:23
  181.3 5.5 %all-to-all-done.6 = f32[4,128,128]{1,2,0:T(8,128)S(1)} async-done(((f32[4,128,128]{1,2,0:T(8,128)}), f32[4,128,128]{1,2,0:T(8,128)S(1)}, u32[]{:S(2)}, u32[]{:S(2)}) %all-to-all-start.6) | async-done | bytes 262176 | tf_op jit(solution)/shard_map/all_to_all | solution.py:23
  187.8 2.9 gather_fusion.6
  191.7 5.6 %all-to-all-start.7 = ((bf16[128,9,128]{2,1,0:T(8,128)(2,1)}), bf16[128,9,128]{2,1,0:T(8,128)(2,1)S(1)}, u32[]{:S(2)}, u32[]{:S(2)}) async-start(bf16[128,9,128]{2,1,0:T(8,128)(2,1)} %convert_element_type.98), calls=%async_computation.7 | async-start | bytes 1048576 | tf_op jit(solution)/shard_map/all_to_all | solution.py:46
  197.3 2.2 collective-permute-start.9
  199.5 4.3 %collective-permute-start.11 = (bf16[128,128]{1,0:T(8,128)(2,1)S(1)}, bf16[128,128]{1,0:T(8,128)(2,1)}, u32[]{:S(2)}, u32[]{:S(2)}) collective-permute-start(bf16[128,128]{1,0:T(8,128)(2,1)S(1)} %get-tuple-element.11), channel_id=1, source_target_pairs={{1,0},{2,1},{3,2},{0,3},{5,4},{6,5},{7,6},{4,7},{9,8},{10,9},{11,1... | collective-permute-start | bytes 98312 | tf_op jit(solution)/shard_map/ppermute | solution.py:56
  205.7 12.2 %all-to-all-done.7 = bf16[128,9,128]{2,1,0:T(8,128)(2,1)S(1)} async-done(((bf16[128,9,128]{2,1,0:T(8,128)(2,1)}), bf16[128,9,128]{2,1,0:T(8,128)(2,1)S(1)}, u32[]{:S(2)}, u32[]{:S(2)}) %all-to-all-start.7) | async-done | bytes 294944 | tf_op jit(solution)/shard_map/all_to_all | solution.py:46
  220.3 3.4 %all-to-all-start.8 = ((f32[4,128,128]{1,2,0:T(8,128)}), f32[4,128,128]{1,2,0:T(8,128)S(1)}, u32[]{:S(2)}, u32[]{:S(2)}) async-start(f32[4,128,128]{1,2,0:T(8,128)} %bitcast.205), calls=%async_computation.8 | async-start | bytes 524288 | tf_op jit(solution)/shard_map/all_to_all | solution.py:23
  225.3 5.5 %all-to-all-done.8 = f32[4,128,128]{1,2,0:T(8,128)S(1)} async-done(((f32[4,128,128]{1,2,0:T(8,128)}), f32[4,128,128]{1,2,0:T(8,128)S(1)}, u32[]{:S(2)}, u32[]{:S(2)}) %all-to-all-start.8) | async-done | bytes 262176 | tf_op jit(solution)/shard_map/all_to_all | solution.py:23
  231.9 2.9 gather_fusion.8
  235.8 5.6 %all-to-all-start.9 = ((bf16[128,9,128]{2,1,0:T(8,128)(2,1)}), bf16[128,9,128]{2,1,0:T(8,128)(2,1)S(1)}, u32[]{:S(2)}, u32[]{:S(2)}) async-start(bf16[128,9,128]{2,1,0:T(8,128)(2,1)} %convert_element_type.101), calls=%async_computation.9 | async-start | bytes 1048576 | tf_op jit(solution)/shard_map/all_to_all | solution.py:46
  241.4 2.2 collective-permute-start.12
  243.6 4.3 %collective-permute-start.14 = (bf16[128,128]{1,0:T(8,128)(2,1)S(1)}, bf16[128,128]{1,0:T(8,128)(2,1)}, u32[]{:S(2)}, u32[]{:S(2)}) collective-permute-start(bf16[128,128]{1,0:T(8,128)(2,1)S(1)} %get-tuple-element.13), channel_id=1, source_target_pairs={{1,0},{2,1},{3,2},{0,3},{5,4},{6,5},{7,6},{4,7},{9,8},{10,9},{11,1... | collective-permute-start | bytes 98312 | tf_op jit(solution)/shard_map/ppermute | solution.py:56
  247.9 2.1 collective-permute-start.13
  250.0 12.0 %all-to-all-done.9 = bf16[128,9,128]{2,1,0:T(8,128)(2,1)S(1)} async-done(((bf16[128,9,128]{2,1,0:T(8,128)(2,1)}), bf16[128,9,128]{2,1,0:T(8,128)(2,1)S(1)}, u32[]{:S(2)}, u32[]{:S(2)}) %all-to-all-start.9) | async-done | bytes 294944 | tf_op jit(solution)/shard_map/all_to_all | solution.py:46
  264.4 3.4 %all-to-all-start.10 = ((f32[4,128,128]{1,2,0:T(8,128)}), f32[4,128,128]{1,2,0:T(8,128)S(1)}, u32[]{:S(2)}, u32[]{:S(2)}) async-start(f32[4,128,128]{1,2,0:T(8,128)} %bitcast.204), calls=%async_computation.10 | async-start | bytes 524288 | tf_op jit(solution)/shard_map/all_to_all | solution.py:23
  269.4 5.6 %all-to-all-done.10 = f32[4,128,128]{1,2,0:T(8,128)S(1)} async-done(((f32[4,128,128]{1,2,0:T(8,128)}), f32[4,128,128]{1,2,0:T(8,128)S(1)}, u32[]{:S(2)}, u32[]{:S(2)}) %all-to-all-start.10) | async-done | bytes 262176 | tf_op jit(solution)/shard_map/all_to_all | solution.py:23
  276.0 2.9 gather_fusion.10
  279.0 26.3 %all_to_all.75 = bf16[128,9,128]{2,1,0:T(8,128)(2,1)} all-to-all(bf16[128,9,128]{2,1,0:T(8,128)(2,1)S(1)} %convert_element_type.104), channel_id=1, replica_groups=mesh['area'=128,'nrn'=4] {'area'}, dimensions={0} | all-to-all | bytes 589824 | tf_op jit(solution)/shard_map/all_to_all | solution.py:46
  308.7 3.4 %all-to-all-start.12 = ((f32[4,128,128]{1,2,0:T(8,128)}), f32[4,128,128]{1,2,0:T(8,128)S(1)}, u32[]{:S(2)}, u32[]{:S(2)}) async-start(f32[4,128,128]{1,2,0:T(8,128)} %bitcast.203), calls=%async_computation.12 | async-start | bytes 524288 | tf_op jit(solution)/shard_map/all_to_all | solution.py:23
  312.2 3.3 %collective-permute-start.15 = (bf16[128,128]{1,0:T(8,128)(2,1)S(1)}, bf16[128,128]{1,0:T(8,128)(2,1)S(1)}, u32[]{:S(2)}, u32[]{:S(2)}) collective-permute-start(bf16[128,128]{1,0:T(8,128)(2,1)S(1)} %get-tuple-element.15), channel_id=1, source_target_pairs={{0,1},{1,2},{2,3},{3,0},{4,5},{5,6},{6,7},{7,4},{8,9},{9,10},{10,1... | collective-permute-start | bytes 98312 | tf_op jit(solution)/shard_map/ppermute | solution.py:54
  315.5 3.2 collective-permute-start.17
  321.9 3.9 %collective-permute-done.16 = bf16[128,128]{1,0:T(8,128)(2,1)S(1)} collective-permute-done((bf16[128,128]{1,0:T(8,128)(2,1)S(1)}, bf16[128,128]{1,0:T(8,128)(2,1)S(1)}, u32[]{:S(2)}, u32[]{:S(2)}) %collective-permute-start.16) | collective-permute-done | bytes 32800 | tf_op jit(solution)/shard_map/ppermute | solution.py:54
  (144 shorter events, 45.0 us)
Async XLA Ops:
  0.0 94.8 %copy-start = (f32[128,512]{1,0:T(8,128)S(1)}, f32[128,512]{1,0:T(8,128)}, u32[]{:S(2)}) copy-start(f32[128,512]{1,0:T(8,128)} %param.11) | copy-start | bytes 786436
  3.8 21.9 %copy-start.1 = (f32[128,4,1152]{2,1,0:T(4,128)S(1)}, f32[128,4,1152]{2,1,0:T(4,128)}, u32[]{:S(2)}) copy-start(f32[128,4,1152]{2,1,0:T(4,128)} %param.12) | copy-start | bytes 7077892
  7.2 39.0 %all-to-all-start = ((bf16[128,9,128]{2,1,0:T(8,128)(2,1)}), bf16[128,9,128]{2,1,0:T(8,128)(2,1)S(1)}, u32[]{:S(2)}, u32[]{:S(2)}) async-start(bf16[128,9,128]{2,1,0:T(8,128)(2,1)} %convert_element_type.88), calls=%async_computation | async-start | bytes 1048576 | tf_op jit(solution)/shard_map/all_to_all | solution.py:46
  46.2 35.8 %all-to-all-start.1 = ((f32[128,4,1152]{2,0,1:T(8,128)}), f32[128,4,1152]{2,0,1:T(8,128)S(1)}, u32[]{:S(2)}, u32[]{:S(2)}) async-start(f32[128,4,1152]{2,0,1:T(8,128)} %copy.14), calls=%async_computation.1 | async-start | bytes 4718592 | tf_op jit(solution)/shard_map/all_to_all | solution.py:40
  50.2 38.9 %collective-permute-start.2 = (bf16[128,128]{1,0:T(8,128)(2,1)S(1)}, bf16[128,128]{1,0:T(8,128)(2,1)}, u32[]{:S(2)}, u32[]{:S(2)}) collective-permute-start(bf16[128,128]{1,0:T(8,128)(2,1)S(1)} %get-tuple-element.6), channel_id=1, source_target_pairs={{1,0},{2,1},{3,2},{0,3},{5,4},{6,5},{7,6},{4,7},{9,8},{10,9},{11,1... | collective-permute-start | bytes 98312 | tf_op jit(solution)/shard_map/ppermute | solution.py:56
  54.8 22.1 %collective-permute-start = (bf16[128,128]{1,0:T(8,128)(2,1)S(1)}, bf16[128,128]{1,0:T(8,128)(2,1)}, u32[]{:S(2)}, u32[]{:S(2)}) collective-permute-start(bf16[128,128]{1,0:T(8,128)(2,1)S(1)} %get-tuple-element.6), channel_id=1, source_target_pairs={{0,1},{1,2},{2,3},{3,0},{4,5},{5,6},{6,7},{7,4},{8,9},{9,10},{10,1... | collective-permute-start | bytes 98312 | tf_op jit(solution)/shard_map/ppermute | solution.py:54
  76.9 12.3 %collective-permute-start.1 = (bf16[128,128]{1,0:T(8,128)(2,1)}, bf16[128,128]{1,0:T(8,128)(2,1)}, u32[]{:S(2)}, u32[]{:S(2)}) collective-permute-start(bf16[128,128]{1,0:T(8,128)(2,1)} %collective-permute-done), channel_id=1, source_target_pairs={{0,1},{1,2},{2,3},{3,0},{4,5},{5,6},{6,7},{7,4},{8,9},{9,10},{10,1... | collective-permute-start | bytes 98312 | tf_op jit(solution)/shard_map/ppermute | solution.py:54
  82.0 7.1 %copy-start.23 = (s32[4]{0:T(128)S(1)}, s32[4]{0:T(128)}, u32[]{:S(2)}) copy-start(s32[4]{0:T(128)} %fusion.48) | copy-start | bytes 52
  82.0 12.8 %copy-start.2 = (f32[128,128]{1,0:T(8,128)S(1)}, f32[128,128]{1,0:T(8,128)}, u32[]{:S(2)}) copy-start(f32[128,128]{1,0:T(8,128)} %param.9) | copy-start | bytes 196612
  82.0 12.8 %copy-start.21 = (f32[128]{0:T(128)S(1)}, f32[128]{0:T(128)}, u32[]{:S(2)}) copy-start(f32[128]{0:T(128)} %param.10) | copy-start | bytes 1540
  85.2 9.5 %all-to-all-start.2 = ((f32[4,128,128]{1,2,0:T(8,128)}), f32[4,128,128]{1,2,0:T(8,128)S(1)}, u32[]{:S(2)}, u32[]{:S(2)}) async-start(f32[4,128,128]{1,2,0:T(8,128)} %bitcast.208), calls=%async_computation.2 | async-start | bytes 524288 | tf_op jit(solution)/shard_map/all_to_all | solution.py:23
  89.1 10.4 %copy-start.22 = (s32[1024]{0:T(1024)}, s32[1024]{0:T(1024)S(1)}, u32[]{:S(2)}) copy-start(s32[1024]{0:T(1024)S(1)} %pad_clamp_fusion.1) | copy-start | bytes 12292
  89.2 11.3 %copy-start.11 = (bf16[3,128,128]{2,1,0:T(8,128)(2,1)}, bf16[3,128,128]{2,1,0:T(8,128)(2,1)S(1)}, u32[]{:S(2)}) copy-start(bf16[3,128,128]{2,1,0:T(8,128)(2,1)S(1)} %slice.51) | copy-start | bytes 294916
  100.5 29.2 %all-to-all-start.3 = ((bf16[128,9,128]{2,1,0:T(8,128)(2,1)}), bf16[128,9,128]{2,1,0:T(8,128)(2,1)S(1)}, u32[]{:S(2)}, u32[]{:S(2)}) async-start(bf16[128,9,128]{2,1,0:T(8,128)(2,1)} %convert_element_type.92), calls=%async_computation.3 | async-start | bytes 1048576 | tf_op jit(solution)/shard_map/all_to_all | solution.py:46
  108.9 6.5 %collective-permute-start.3 = (bf16[128,128]{1,0:T(8,128)(2,1)S(1)}, bf16[128,128]{1,0:T(8,128)(2,1)}, u32[]{:S(2)}, u32[]{:S(2)}) collective-permute-start(bf16[128,128]{1,0:T(8,128)(2,1)S(1)} %get-tuple-element.7), channel_id=1, source_target_pairs={{0,1},{1,2},{2,3},{3,0},{4,5},{5,6},{6,7},{7,4},{8,9},{9,10},{10,1... | collective-permute-start | bytes 98312 | tf_op jit(solution)/shard_map/ppermute | solution.py:54
  111.2 24.3 %collective-permute-start.5 = (bf16[128,128]{1,0:T(8,128)(2,1)S(1)}, bf16[128,128]{1,0:T(8,128)(2,1)}, u32[]{:S(2)}, u32[]{:S(2)}) collective-permute-start(bf16[128,128]{1,0:T(8,128)(2,1)S(1)} %get-tuple-element.7), channel_id=1, source_target_pairs={{1,0},{2,1},{3,2},{0,3},{5,4},{6,5},{7,6},{4,7},{9,8},{10,9},{11,1... | collective-permute-start | bytes 98312 | tf_op jit(solution)/shard_map/ppermute | solution.py:56
  115.5 20.0 %collective-permute-start.4 = (bf16[128,128]{1,0:T(8,128)(2,1)}, bf16[128,128]{1,0:T(8,128)(2,1)}, u32[]{:S(2)}, u32[]{:S(2)}) collective-permute-start(bf16[128,128]{1,0:T(8,128)(2,1)} %collective-permute-done.3), channel_id=1, source_target_pairs={{0,1},{1,2},{2,3},{3,0},{4,5},{5,6},{6,7},{7,4},{8,9},{9,10},{10,1... | collective-permute-start | bytes 98312 | tf_op jit(solution)/shard_map/ppermute | solution.py:54
  129.8 5.6 %copy-start.4 = (f32[128,128]{1,0:T(8,128)S(1)}, f32[128,128]{1,0:T(8,128)}, u32[]{:S(2)}) copy-start(f32[128,128]{1,0:T(8,128)} %copy-done.3) | copy-start | bytes 196612
  129.8 5.6 %copy-start.12 = (bf16[3,128,128]{2,1,0:T(8,128)(2,1)S(1)}, bf16[3,128,128]{2,1,0:T(8,128)(2,1)}, u32[]{:S(2)}) copy-start(bf16[3,128,128]{2,1,0:T(8,128)(2,1)} %copy-done.11) | copy-start | bytes 294916
  132.0 10.6 %all-to-all-start.4 = ((f32[4,128,128]{1,2,0:T(8,128)}), f32[4,128,128]{1,2,0:T(8,128)S(1)}, u32[]{:S(2)}, u32[]{:S(2)}) async-start(f32[4,128,128]{1,2,0:T(8,128)} %bitcast.207), calls=%async_computation.4 | async-start | bytes 524288 | tf_op jit(solution)/shard_map/all_to_all | solution.py:23
  135.4 12.0 %copy-start.13 = (bf16[3,128,128]{2,1,0:T(8,128)(2,1)}, bf16[3,128,128]{2,1,0:T(8,128)(2,1)S(1)}, u32[]{:S(2)}) copy-start(bf16[3,128,128]{2,1,0:T(8,128)(2,1)S(1)} %fusion.45) | copy-start | bytes 294916
  147.4 26.5 %all-to-all-start.5 = ((bf16[128,9,128]{2,1,0:T(8,128)(2,1)}), bf16[128,9,128]{2,1,0:T(8,128)(2,1)S(1)}, u32[]{:S(2)}, u32[]{:S(2)}) async-start(bf16[128,9,128]{2,1,0:T(8,128)(2,1)} %convert_element_type.95), calls=%async_computation.5 | async-start | bytes 1048576 | tf_op jit(solution)/shard_map/all_to_all | solution.py:46
  153.2 6.5 %collective-permute-start.6 = (bf16[128,128]{1,0:T(8,128)(2,1)S(1)}, bf16[128,128]{1,0:T(8,128)(2,1)}, u32[]{:S(2)}, u32[]{:S(2)}) collective-permute-start(bf16[128,128]{1,0:T(8,128)(2,1)S(1)} %get-tuple-element.9), channel_id=1, source_target_pairs={{0,1},{1,2},{2,3},{3,0},{4,5},{5,6},{6,7},{7,4},{8,9},{9,10},{10,1... | collective-permute-start | bytes 98312 | tf_op jit(solution)/shard_map/ppermute | solution.py:54
  155.4 24.3 %collective-permute-start.8 = (bf16[128,128]{1,0:T(8,128)(2,1)S(1)}, bf16[128,128]{1,0:T(8,128)(2,1)}, u32[]{:S(2)}, u32[]{:S(2)}) collective-permute-start(bf16[128,128]{1,0:T(8,128)(2,1)S(1)} %get-tuple-element.9), channel_id=1, source_target_pairs={{1,0},{2,1},{3,2},{0,3},{5,4},{6,5},{7,6},{4,7},{9,8},{10,9},{11,1... | collective-permute-start | bytes 98312 | tf_op jit(solution)/shard_map/ppermute | solution.py:56
  159.7 20.0 %collective-permute-start.7 = (bf16[128,128]{1,0:T(8,128)(2,1)}, bf16[128,128]{1,0:T(8,128)(2,1)}, u32[]{:S(2)}, u32[]{:S(2)}) collective-permute-start(bf16[128,128]{1,0:T(8,128)(2,1)} %collective-permute-done.6), channel_id=1, source_target_pairs={{0,1},{1,2},{2,3},{3,0},{4,5},{5,6},{6,7},{7,4},{8,9},{9,10},{10,1... | collective-permute-start | bytes 98312 | tf_op jit(solution)/shard_map/ppermute | solution.py:54
  174.0 5.6 %copy-start.6 = (f32[128,128]{1,0:T(8,128)S(1)}, f32[128,128]{1,0:T(8,128)}, u32[]{:S(2)}) copy-start(f32[128,128]{1,0:T(8,128)} %copy-done.5) | copy-start | bytes 196612
  174.1 5.6 %copy-start.14 = (bf16[3,128,128]{2,1,0:T(8,128)(2,1)S(1)}, bf16[3,128,128]{2,1,0:T(8,128)(2,1)}, u32[]{:S(2)}) copy-start(bf16[3,128,128]{2,1,0:T(8,128)(2,1)} %copy-done.13) | copy-start | bytes 294916
  176.2 10.6 %all-to-all-start.6 = ((f32[4,128,128]{1,2,0:T(8,128)}), f32[4,128,128]{1,2,0:T(8,128)S(1)}, u32[]{:S(2)}, u32[]{:S(2)}) async-start(f32[4,128,128]{1,2,0:T(8,128)} %bitcast.206), calls=%async_computation.6 | async-start | bytes 524288 | tf_op jit(solution)/shard_map/all_to_all | solution.py:23
  179.7 12.0 %copy-start.15 = (bf16[3,128,128]{2,1,0:T(8,128)(2,1)}, bf16[3,128,128]{2,1,0:T(8,128)(2,1)S(1)}, u32[]{:S(2)}) copy-start(bf16[3,128,128]{2,1,0:T(8,128)(2,1)S(1)} %fusion.44) | copy-start | bytes 294916
  191.7 26.3 %all-to-all-start.7 = ((bf16[128,9,128]{2,1,0:T(8,128)(2,1)}), bf16[128,9,128]{2,1,0:T(8,128)(2,1)S(1)}, u32[]{:S(2)}, u32[]{:S(2)}) async-start(bf16[128,9,128]{2,1,0:T(8,128)(2,1)} %convert_element_type.98), calls=%async_computation.7 | async-start | bytes 1048576 | tf_op jit(solution)/shard_map/all_to_all | solution.py:46
  197.3 6.5 %collective-permute-start.9 = (bf16[128,128]{1,0:T(8,128)(2,1)S(1)}, bf16[128,128]{1,0:T(8,128)(2,1)}, u32[]{:S(2)}, u32[]{:S(2)}) collective-permute-start(bf16[128,128]{1,0:T(8,128)(2,1)S(1)} %get-tuple-element.11), channel_id=1, source_target_pairs={{0,1},{1,2},{2,3},{3,0},{4,5},{5,6},{6,7},{7,4},{8,9},{9,10},{10,1... | collective-permute-start | bytes 98312 | tf_op jit(solution)/shard_map/ppermute | solution.py:54
  199.5 24.3 %collective-permute-start.11 = (bf16[128,128]{1,0:T(8,128)(2,1)S(1)}, bf16[128,128]{1,0:T(8,128)(2,1)}, u32[]{:S(2)}, u32[]{:S(2)}) collective-permute-start(bf16[128,128]{1,0:T(8,128)(2,1)S(1)} %get-tuple-element.11), channel_id=1, source_target_pairs={{1,0},{2,1},{3,2},{0,3},{5,4},{6,5},{7,6},{4,7},{9,8},{10,9},{11,1... | collective-permute-start | bytes 98312 | tf_op jit(solution)/shard_map/ppermute | solution.py:56
  203.8 20.0 %collective-permute-start.10 = (bf16[128,128]{1,0:T(8,128)(2,1)}, bf16[128,128]{1,0:T(8,128)(2,1)}, u32[]{:S(2)}, u32[]{:S(2)}) collective-permute-start(bf16[128,128]{1,0:T(8,128)(2,1)} %collective-permute-done.9), channel_id=1, source_target_pairs={{0,1},{1,2},{2,3},{3,0},{4,5},{5,6},{6,7},{7,4},{8,9},{9,10},{10,1... | collective-permute-start | bytes 98312 | tf_op jit(solution)/shard_map/ppermute | solution.py:54
  218.1 5.6 %copy-start.8 = (f32[128,128]{1,0:T(8,128)S(1)}, f32[128,128]{1,0:T(8,128)}, u32[]{:S(2)}) copy-start(f32[128,128]{1,0:T(8,128)} %copy-done.7) | copy-start | bytes 196612
  218.1 5.6 %copy-start.16 = (bf16[3,128,128]{2,1,0:T(8,128)(2,1)S(1)}, bf16[3,128,128]{2,1,0:T(8,128)(2,1)}, u32[]{:S(2)}) copy-start(bf16[3,128,128]{2,1,0:T(8,128)(2,1)} %copy-done.15) | copy-start | bytes 294916
  220.3 10.6 %all-to-all-start.8 = ((f32[4,128,128]{1,2,0:T(8,128)}), f32[4,128,128]{1,2,0:T(8,128)S(1)}, u32[]{:S(2)}, u32[]{:S(2)}) async-start(f32[4,128,128]{1,2,0:T(8,128)} %bitcast.205), calls=%async_computation.8 | async-start | bytes 524288 | tf_op jit(solution)/shard_map/all_to_all | solution.py:23
  223.8 12.0 %copy-start.17 = (bf16[3,128,128]{2,1,0:T(8,128)(2,1)}, bf16[3,128,128]{2,1,0:T(8,128)(2,1)S(1)}, u32[]{:S(2)}) copy-start(bf16[3,128,128]{2,1,0:T(8,128)(2,1)S(1)} %fusion.43) | copy-start | bytes 294916
  235.8 26.3 %all-to-all-start.9 = ((bf16[128,9,128]{2,1,0:T(8,128)(2,1)}), bf16[128,9,128]{2,1,0:T(8,128)(2,1)S(1)}, u32[]{:S(2)}, u32[]{:S(2)}) async-start(bf16[128,9,128]{2,1,0:T(8,128)(2,1)} %convert_element_type.101), calls=%async_computation.9 | async-start | bytes 1048576 | tf_op jit(solution)/shard_map/all_to_all | solution.py:46
  241.4 6.5 %collective-permute-start.12 = (bf16[128,128]{1,0:T(8,128)(2,1)S(1)}, bf16[128,128]{1,0:T(8,128)(2,1)}, u32[]{:S(2)}, u32[]{:S(2)}) collective-permute-start(bf16[128,128]{1,0:T(8,128)(2,1)S(1)} %get-tuple-element.13), channel_id=1, source_target_pairs={{0,1},{1,2},{2,3},{3,0},{4,5},{5,6},{6,7},{7,4},{8,9},{9,10},{10,1... | collective-permute-start | bytes 98312 | tf_op jit(solution)/shard_map/ppermute | solution.py:54
  243.6 24.3 %collective-permute-start.14 = (bf16[128,128]{1,0:T(8,128)(2,1)S(1)}, bf16[128,128]{1,0:T(8,128)(2,1)}, u32[]{:S(2)}, u32[]{:S(2)}) collective-permute-start(bf16[128,128]{1,0:T(8,128)(2,1)S(1)} %get-tuple-element.13), channel_id=1, source_target_pairs={{1,0},{2,1},{3,2},{0,3},{5,4},{6,5},{7,6},{4,7},{9,8},{10,9},{11,1... | collective-permute-start | bytes 98312 | tf_op jit(solution)/shard_map/ppermute | solution.py:56
  247.9 20.0 %collective-permute-start.13 = (bf16[128,128]{1,0:T(8,128)(2,1)}, bf16[128,128]{1,0:T(8,128)(2,1)}, u32[]{:S(2)}, u32[]{:S(2)}) collective-permute-start(bf16[128,128]{1,0:T(8,128)(2,1)} %collective-permute-done.12), channel_id=1, source_target_pairs={{0,1},{1,2},{2,3},{3,0},{4,5},{5,6},{6,7},{7,4},{8,9},{9,10},{10,1... | collective-permute-start | bytes 98312 | tf_op jit(solution)/shard_map/ppermute | solution.py:54
  262.2 5.6 %copy-start.10 = (f32[128,128]{1,0:T(8,128)S(1)}, f32[128,128]{1,0:T(8,128)}, u32[]{:S(2)}) copy-start(f32[128,128]{1,0:T(8,128)} %copy-done.9) | copy-start | bytes 196612
  264.4 10.5 %all-to-all-start.10 = ((f32[4,128,128]{1,2,0:T(8,128)}), f32[4,128,128]{1,2,0:T(8,128)S(1)}, u32[]{:S(2)}, u32[]{:S(2)}) async-start(f32[4,128,128]{1,2,0:T(8,128)} %bitcast.204), calls=%async_computation.10 | async-start | bytes 524288 | tf_op jit(solution)/shard_map/all_to_all | solution.py:23
  306.6 20.2 %copy-start.20 = (f32[128,128]{1,0:T(8,128)S(1)}, f32[128,128]{1,0:T(8,128)}, u32[]{:S(2)}) copy-start(f32[128,128]{1,0:T(8,128)} %copy-done.19) | copy-start | bytes 196612
  308.7 17.8 %all-to-all-start.12 = ((f32[4,128,128]{1,2,0:T(8,128)}), f32[4,128,128]{1,2,0:T(8,128)S(1)}, u32[]{:S(2)}, u32[]{:S(2)}) async-start(f32[4,128,128]{1,2,0:T(8,128)} %bitcast.203), calls=%async_computation.12 | async-start | bytes 524288 | tf_op jit(solution)/shard_map/all_to_all | solution.py:23
  312.2 7.8 %collective-permute-start.15 = (bf16[128,128]{1,0:T(8,128)(2,1)S(1)}, bf16[128,128]{1,0:T(8,128)(2,1)S(1)}, u32[]{:S(2)}, u32[]{:S(2)}) collective-permute-start(bf16[128,128]{1,0:T(8,128)(2,1)S(1)} %get-tuple-element.15), channel_id=1, source_target_pairs={{0,1},{1,2},{2,3},{3,0},{4,5},{5,6},{6,7},{7,4},{8,9},{9,10},{10,1... | collective-permute-start | bytes 98312 | tf_op jit(solution)/shard_map/ppermute | solution.py:54
  315.5 6.4 %collective-permute-start.17 = (bf16[128,128]{1,0:T(8,128)(2,1)S(1)}, bf16[128,128]{1,0:T(8,128)(2,1)S(1)}, u32[]{:S(2)}, u32[]{:S(2)}) collective-permute-start(bf16[128,128]{1,0:T(8,128)(2,1)S(1)} %get-tuple-element.15), channel_id=1, source_target_pairs={{1,0},{2,1},{3,2},{0,3},{5,4},{6,5},{7,6},{4,7},{9,8},{10,9},{11,1... | collective-permute-start | bytes 98312 | tf_op jit(solution)/shard_map/ppermute | solution.py:56
  320.0 5.9 %collective-permute-start.16 = (bf16[128,128]{1,0:T(8,128)(2,1)S(1)}, bf16[128,128]{1,0:T(8,128)(2,1)S(1)}, u32[]{:S(2)}, u32[]{:S(2)}) collective-permute-start(bf16[128,128]{1,0:T(8,128)(2,1)S(1)} %collective-permute-done.15), channel_id=1, source_target_pairs={{0,1},{1,2},{2,3},{3,0},{4,5},{5,6},{6,7},{7,4},{8,9},{9,10},{10,1... | collective-permute-start | bytes 98312 | tf_op jit(solution)/shard_map/ppermute | solution.py:54
  (6 other events, 8.8 us)
